TPU v7x, 256 devices: a whole 4x4x8 slice. The times are simulated.
256 devices in a mesh: rep: 16 (over z, y_hi), tp: 16 (over y_lo, x, core).
Axes of the slice: x: 4, y: 4 (y_hi: 2, y_lo: 2; y = y_hi * 2 + y_lo), z: 8, core: 2. Of those that a mesh axis runs over, the one named last changes fastest.
Arguments:
- weights: bfloat16 [14336, 4096], P('tp'), may hold values from -0.046875 to 0.046875
- hidden_pool: bfloat16 [16, 512, 14336], P('rep', None, 'tp'), may hold values from -6 to 6
- target_pool: bfloat16 [16, 512, 4096], P('rep', None, 'tp'), may hold values from -6 to 6
- token_rows: int32 [16, 2, 256], P('rep'), may hold values from 0 to 511
- fragment: int32 [1], replicated, may hold values from 0 to 15
- outer_momentum: float32 [14336, 256], P('tp'), may hold values from -0.005859375 to 0.005859375
Outputs:
- new_momentum: float32 [14336, 256], P('tp')
- new_global: float32 [14336, 256], P('tp')
- local_fragment: bfloat16 [16, 14336, 256], P('rep', 'tp')
- last_residual: float32 [16, 4096, 256], P('rep', 'tp')
All inputs are finite; a program needn't handle non-finite values.
Results may differ from a plain program's by a relative error of at most 0.033.
Values may be sent and summed in bfloat16 or wider, within the bound.
A program may use at most 192 MiB of HBM per device.

v0:
```python
import jax
import jax.numpy as jnp
from jax import lax
from jax.sharding import PartitionSpec as P

BETA_ONE = 0.9
BETA_TWO = 0.95
INNER_RATE = 0.001
DECAY_RATE = 0.1
ADAM_EPS = 0.001
OUTER_RATE = 0.7
OUTER_MOMENTUM = 0.9
MIX_KEEP = 0.5


def adam_update(master, first, second, grad, count):
    first = BETA_ONE * first + (1.0 - BETA_ONE) * grad
    second = BETA_TWO * second + (1.0 - BETA_TWO) * grad * grad
    ratio = (
        first / (1.0 - BETA_ONE**count) / (jnp.sqrt(second / (1.0 - BETA_TWO**count)) + ADAM_EPS)
    )
    master = master - INNER_RATE * (ratio + DECAY_RATE * master)
    return (master, first, second)


def body(weights, hidden_pool, target_pool, token_rows, fragment, outer_momentum):
    width = outer_momentum.shape[1]
    feature_rows = target_pool.shape[2]
    tokens = token_rows.shape[2]
    steps_all = token_rows.shape[1]
    start = fragment[0] * width
    anchor = lax.dynamic_slice_in_dim(weights, start, width, 1).astype(jnp.float32)
    master = weights.astype(jnp.float32)
    first = jnp.zeros_like(master)
    second = jnp.zeros_like(master)
    synced = anchor
    residual_rows_out = jnp.zeros((feature_rows, tokens), jnp.float32)
    for step in range(steps_all):
        rows = token_rows[0, step]
        hidden = jnp.take(hidden_pool[0], rows, axis=0)
        current = master.astype(jnp.bfloat16)
        outputs_t = lax.psum_scatter(
            jnp.einsum("fd,tf->dt", current, hidden, preferred_element_type=jnp.float32).astype(
                jnp.bfloat16
            ),
            "tp",
            scatter_dimension=0,
            tiled=True,
        ).astype(jnp.float32)
        target = jnp.take(target_pool[0], rows, axis=0)
        difference_t = outputs_t - target.T.astype(jnp.float32)
        slope_t = (difference_t / tokens).astype(jnp.bfloat16)
        grad = jnp.einsum(
            "tf,dt->fd",
            hidden,
            lax.all_gather(slope_t, "tp", axis=0, tiled=True),
            preferred_element_type=jnp.float32,
        )
        if step == steps_all - 1:
            residual_rows_out = difference_t
        master, first, second = adam_update(master, first, second, grad, step + 1)
        if step == steps_all - 2:
            synced = lax.dynamic_slice_in_dim(master, start, width, 1)
    final_local = lax.dynamic_slice_in_dim(master, start, width, 1)
    drift = (anchor - synced).astype(jnp.bfloat16).astype(jnp.float32)
    replicas = lax.axis_size("rep")
    mean_drift = lax.psum(drift.astype(jnp.bfloat16), "rep").astype(jnp.float32) / replicas
    new_momentum = OUTER_MOMENTUM * outer_momentum + mean_drift
    new_global = anchor - OUTER_RATE * (mean_drift + OUTER_MOMENTUM * new_momentum)
    local_fragment = (MIX_KEEP * final_local + (1.0 - MIX_KEEP) * new_global).astype(jnp.bfloat16)
    return (new_momentum, new_global, local_fragment[None], residual_rows_out[None])


def solution(mesh):
    in_specs = (
        P("tp", None),
        P("rep", None, "tp"),
        P("rep", None, "tp"),
        P("rep", None, None),
        P(),
        P("tp", None),
    )
    out_specs = (P("tp", None), P("tp", None), P("rep", "tp", None), P("rep", "tp", None))
    return jax.shard_map(body, mesh=mesh, in_specs=in_specs, out_specs=out_specs, check_vma=False)
```

profile of v0, /device:TPU:2, one launch (start us, length us, event | category | flops | bytes accessed | tf_op | source)
XLA Modules:
  0.0 429.9 jit_solution(8701917642395058919)
XLA Ops:
  7.2 0.0 copy-start
  7.2 0.0 copy-start.2
  7.2 0.0 reduce-scatter.3.cloned.1.call-start
  7.2 0.8 fusion.30
  8.1 0.3 copy-done
  8.4 1.2 gather_fusion
  9.6 7.6 %fusion.9 = bf16[4096,256]{1,0:T(8,128)(2,1)} fusion(bf16[896,4096]{1,0:T(8,128)(2,1)} %param.10, bf16[256,896]{1,0:T(8,128)(2,1)S(1)} %gather_fusion, pred[256]{0:T(512)(128)(4,1)S(1)} %compare_and_fusion.1), kind=kOutput, calls=%fused_computation.18 | convolution fusion | flops 1880326144 | bytes 9896192 | tf_op jit(solution)/shard_map/fd,tf->dt/dot_general | solution.py:43
  17.2 0.0 reduce-scatter.3.cloned.1.call-update
  17.2 0.0 all-gather.3.cloned.1.call-start
  17.3 0.0 copy-done.2
  17.3 1.2 gather_fusion.1
  18.4 0.1 copy.10
  18.6 63.7 %reduce-scatter.3.cloned.1.call-done = bf16[256,256]{1,0:T(8,128)(2,1)} async-done(((bf16[4096,256]{1,0:T(8,128)(2,1)}), bf16[256,256]{1,0:T(8,128)(2,1)}) %reduce-scatter.3.cloned.1.call-update) | async-done | bytes 131088 | tf_op jit(solution)/shard_map/reduce_scatter | solution.py:42
  82.2 1.6 fusion.21
  83.8 0.0 all-gather.3.cloned.1.call-update
  83.9 0.2 reduce-scatter.5.cloned.1.call-start
  84.1 1.2 gather_fusion.2
  85.3 38.0 %all-gather.3.cloned.1.call-done = bf16[4096,256]{1,0:T(8,128)(2,1)} async-done(((bf16[256,256]{1,0:T(8,128)(2,1)}), bf16[4096,256]{1,0:T(8,128)(2,1)}) %all-gather.3.cloned.1.call-update) | async-done | bytes 2097168 | tf_op jit(solution)/shard_map/all_gather | solution.py:56
  123.4 21.8 %broadcast_multiply_fusion = (f32[896,4096]{1,0:T(8,128)}, f32[896,4096]{1,0:T(8,128)}, f32[896,4096]{1,0:T(8,128)}) fusion(bf16[896,4096]{1,0:T(8,128)(2,1)} %param.10, bf16[4096,256]{1,0:T(8,128)(2,1)} %all-gather.3.cloned.1.call-done, bf16[256,896]{1,0:T(8,128)(2,1)S(1)} %gather_fusion, pred[256]{0:T(512)(128)(4,1)S(1)} %compare_and_fusion.1), kind=kOutput, calls=%fused_computation.14 | convolution fusion | flops 1919647744 | bytes 53936384 | tf_op jit(solution)/shard_map/tf,dt->fd/dot_general | solution.py:53
  145.1 9.0 %fusion.6 = bf16[4096,256]{1,0:T(8,128)(2,1)} fusion(f32[896,4096]{1,0:T(8,128)} %get-tuple-element.10, bf16[256,896]{1,0:T(8,128)(2,1)S(1)} %gather_fusion.2, pred[256]{0:T(512)(128)(4,1)S(1)} %compare_and_fusion), kind=kOutput, calls=%fused_computation.16 | convolution fusion | flops 1883996160 | bytes 17236224 | tf_op jit(solution)/shard_map/fd,tf->dt/dot_general | solution.py:43
  154.1 0.0 reduce-scatter.5.cloned.1.call-update
  154.1 0.0 all-gather.5.cloned.1.call-start
  154.2 1.2 gather_fusion.3
  155.3 0.1 copy.11
  155.4 61.3 %reduce-scatter.5.cloned.1.call-done = bf16[256,256]{1,0:T(8,128)(2,1)} async-done(((bf16[4096,256]{1,0:T(8,128)(2,1)}), bf16[256,256]{1,0:T(8,128)(2,1)}) %reduce-scatter.5.cloned.1.call-update) | async-done | bytes 131088 | tf_op jit(solution)/shard_map/reduce_scatter | solution.py:42
  216.7 1.7 fusion.22
  218.4 0.0 all-gather.5.cloned.1.call-update
  218.4 0.3 all-reduce.2.cloned.1.call-start
  219.4 2.2 fusion.10
  221.5 0.0 all-reduce.2.cloned.1.call-update
  221.6 36.1 %all-gather.5.cloned.1.call-done = bf16[4096,256]{1,0:T(8,128)(2,1)} async-done(((bf16[256,256]{1,0:T(8,128)(2,1)}), bf16[4096,256]{1,0:T(8,128)(2,1)}) %all-gather.5.cloned.1.call-update) | async-done | bytes 2097168 | tf_op jit(solution)/shard_map/all_gather | solution.py:56
  257.7 0.0 copy-start.3
  257.7 0.0 copy-start.1
  257.7 16.3 %broadcast_multiply_fusion.1 = (f32[896,4096]{1,0:T(8,128)}, f32[896,4096]{1,0:T(8,128)}) fusion(f32[896,4096]{1,0:T(8,128)} %get-tuple-element.17, bf16[4096,256]{1,0:T(8,128)(2,1)} %all-gather.5.cloned.1.call-done, bf16[256,896]{1,0:T(8,128)(2,1)S(1)} %gather_fusion.2, pred[256]{0:T(512)(128)(4,1)S(1)} %compare_and_fusion), kind=kOutput, calls=%fused_computation.15 | convolution fusion | flops 1908637696 | bytes 46596352 | tf_op jit(solution)/shard_map/tf,dt->fd/dot_general | solution.py:53
  274.0 145.4 %all-reduce.2.cloned.1.call-done = bf16[896,256]{1,0:T(8,128)(2,1)} async-done(((bf16[896,256]{1,0:T(8,128)(2,1)}), bf16[896,256]{1,0:T(8,128)(2,1)}) %all-reduce.2.cloned.1.call-update) | async-done | bytes 458768 | tf_op jit(solution)/shard_map/psum | solution.py:67
  419.5 0.0 copy-done.3
  419.5 3.9 fusion.19
  423.4 0.0 copy-done.1
  (5 shorter events, 0.0 us)
Async XLA Ops:
  7.2 1.2 copy-start
  7.2 10.1 %copy-start.2 = (bf16[1,512,256]{2,1,0:T(8,128)(2,1)S(1)}, bf16[1,512,256]{2,1,0:T(8,128)(2,1)}, u32[]{:S(2)}) copy-start(bf16[1,512,256]{2,1,0:T(8,128)(2,1)} %param.12) | copy-start | bytes 786436
  7.2 75.0 %reduce-scatter.3.cloned.1.call-start = ((), (), s32[]{:S(2)}) async-start(), calls=%async_computation.2 | async-start | bytes 2228224 | tf_op jit(solution)/shard_map/reduce_scatter | solution.py:42
  17.2 106.1 %all-gather.3.cloned.1.call-start = ((), (), s32[]{:S(2)}) async-start(), calls=%async_computation.3 | async-start | bytes 2228224 | tf_op jit(solution)/shard_map/all_gather | solution.py:56
  83.9 132.9 %reduce-scatter.5.cloned.1.call-start = ((), (), s32[]{:S(2)}) async-start(), calls=%async_computation.5 | async-start | bytes 2228224 | tf_op jit(solution)/shard_map/reduce_scatter | solution.py:42
  154.1 103.6 %all-gather.5.cloned.1.call-start = ((), (), s32[]{:S(2)}) async-start(), calls=%async_computation.6 | async-start | bytes 2228224 | tf_op jit(solution)/shard_map/all_gather | solution.py:56
  218.4 201.0 %all-reduce.2.cloned.1.call-start = ((), (), s32[]{:S(2)}) async-start(), calls=%async_computation.4 | async-start | bytes 917504 | tf_op jit(solution)/shard_map/psum | solution.py:67
  257.7 161.8 %copy-start.3 = (f32[896,256]{1,0:T(8,128)S(1)}, f32[896,256]{1,0:T(8,128)}, u32[]{:S(2)}) copy-start(f32[896,256]{1,0:T(8,128)} %param.15) | copy-start | bytes 2752516
  257.7 165.7 %copy-start.1 = (bf16[1,512,896]{2,1,0:T(8,128)(2,1)S(1)}, bf16[1,512,896]{2,1,0:T(8,128)(2,1)}, u32[]{:S(2)}) copy-start(bf16[1,512,896]{2,1,0:T(8,128)(2,1)} %param.11) | copy-start | bytes 2752516
Sparse Core Ops, SparseCore 0:
  17.4 64.8 reduce-scatter.2
  84.6 38.6 all-gather.2
  154.3 62.4 reduce-scatter.4
  219.0 38.6 all-gather.4
  260.8 158.6 all-reduce.1
where the time goes:
time: 430 us
  waiting for transfers between devices  345 us (80%)
  matrix products  54.7 us (13%)
  between operations  14.5 us (3%)
  other arithmetic  9.44 us (2%)
  local copies, waits for them, and re-layouts  6.03 us (1%)
    psum x1, waiting for transfers between devices, body(): lax.psum(drift.astype(jnp.bfloat16), 'rep').astype(jnp.float32) / replicas  145 us
    reduce_scatter x2, waiting for transfers between devices, body(): lax.psum_scatter(jnp.einsum('fd,tf->dt', current, hidden, preferred_eleme...  125 us
    all_gather x2, waiting for transfers between devices, body(): lax.all_gather(slope_t, 'tp', axis=0, tiled=True)  74.2 us
    dot_general x2, matrix products, body(): jnp.einsum('tf,dt->fd', hidden, lax.all_gather(slope_t, 'tp', axis=0, til...  38.1 us
    dot_general x2, matrix products, body(): jnp.einsum('fd,tf->dt', current, hidden, preferred_element_type=jnp.float32)  16.6 us
  transfers between devices with their start and end apart: 5, of which 5 were waited for; matrix products, arithmetic and copies ran while one was open for 5% of the time, Pallas kernels for 0%

commit v1 on v0

v1 whole, which is shorter than its diff:
```python
import functools

import jax
import jax.numpy as jnp
from jax import lax
from jax.experimental import pallas as pl
from jax.experimental.pallas import tpu as pltpu
from jax.sharding import PartitionSpec as P

BETA_ONE = 0.9
BETA_TWO = 0.95
INNER_RATE = 0.001
DECAY_RATE = 0.1
ADAM_EPS = 0.001
OUTER_RATE = 0.7
OUTER_MOMENTUM = 0.9
MIX_KEEP = 0.5

MESH = pl.DeviceIdType.MESH
F32 = jnp.float32
BF16 = jnp.bfloat16

NX = 4
NCHIP = 8
NTP = 16
NZ = 8
LANES = 128


def dot(a, b, ca=1, cb=0):
    return lax.dot_general(a, b, (((ca,), (cb,)), ((), ())), preferred_element_type=F32)


def recip(x):
    r = pl.reciprocal(x, approx=True)
    return r * (2.0 - x * r)


def kernel(
    w_hbm, pool_hbm, tpool_hbm, rows_ref, frag_ref, mom_hbm,
    nm_ref, ng_ref, lf_ref, res_ref,
    w_v, pool_v, tpool_v, mom_v,
    h1, h2, ht1, ht2, tgt,
    keep, sibs, sibr, rss, rsr,
    slope0, slope1,
    g1f, synced, drift0, drift1, fpart, frecv, fslope, final,
    zrecv, ysend, yrecv, total,
    w_sem, in_sem,
    sib_s, sib_r, rs_s, rs_r, ag_s, ag_r, agd_s, agd_r,
    f1_s, f1_r, f2_s, f2_r, z1_s, z1_r, y_s, y_r, z2_s, z2_r,
):
    tokens = rows_ref.shape[1]
    pool = pool_v.shape[0]
    depth = w_v.shape[1]
    zrows = depth // NZ
    ftok = tokens // NTP

    me = lax.axis_index("tp")
    core = lax.rem(me, 2)
    chip = lax.div(me, 2)
    cy = lax.div(chip, NX)
    cx = lax.rem(chip, NX)
    rep = lax.axis_index("rep")
    rz = lax.div(rep, 2)
    ry = lax.rem(rep, 2)
    sibling = chip * 2 + 1 - core
    frag = frag_ref[0]
    slopes = (slope0, slope1)
    drifts = (drift0, drift1)

    def chip_at(s):
        return lax.rem(cy + lax.div(s, NX), 2) * NX + lax.rem(cx + lax.rem(s, NX), NX)

    def chip_from(s):
        return lax.rem(cy + lax.div(s, NX), 2) * NX + lax.rem(cx + NX - lax.rem(s, NX), NX)

    def rep_at(s):
        return lax.rem(rz + s, NZ) * 2 + ry

    def loop(lo, hi, body):
        def step(i, carry):
            body(i)
            return carry

        lax.fori_loop(lo, hi, step, 0)

    def w_copy(c, s, j):
        slot = (chip_at(s) * 2 + j) * 2 + c
        return pltpu.make_async_copy(
            w_hbm.at[:, pl.ds(pl.multiple_of(slot * LANES, LANES), LANES)],
            w_v.at[slot],
            w_sem.at[c, s, j],
        )

    pool_copy = pltpu.make_async_copy(pool_hbm.at[0], pool_v, in_sem.at[0])
    tpool_copy = pltpu.make_async_copy(tpool_hbm.at[0], tpool_v, in_sem.at[1])
    mom_copy = pltpu.make_async_copy(mom_hbm, mom_v, in_sem.at[2])
    pool_copy.start()
    for c in range(2):

        def start_w(s, c=c):
            w_copy(c, s, 0).start()
            w_copy(c, s, 1).start()

        loop(0, NCHIP, start_w)
    tpool_copy.start()
    mom_copy.start()

    barrier = pltpu.get_barrier_semaphore()

    def greet_tp(i):
        pl.semaphore_signal(
            barrier, inc=1, device_id={"tp": lax.rem(me + i, NTP)}, device_id_type=MESH
        )

    def greet_z(i):
        pl.semaphore_signal(barrier, inc=1, device_id={"rep": rep_at(i)}, device_id_type=MESH)

    loop(1, NTP, greet_tp)
    loop(1, NZ, greet_z)
    pl.semaphore_signal(barrier, inc=1, device_id={"rep": rz * 2 + 1 - ry}, device_id_type=MESH)

    def picks(k):
        at = lax.broadcasted_iota(jnp.int32, (pool, tokens), 0)
        return jnp.where(at == rows_ref[pl.ds(k, 1), :], 1.0, 0.0).astype(BF16)

    pool_copy.wait()
    h1[...] = dot(picks(0), pool_v[...], 0, 0).astype(BF16)

    pl.semaphore_wait(barrier, NTP - 1 + NZ)

    def sib_copy(u, s):
        return pltpu.make_async_remote_copy(
            src_ref=sibs.at[u, s], dst_ref=sibr.at[u, s],
            send_sem=sib_s.at[u, s], recv_sem=sib_r.at[u, s],
            device_id={"tp": sibling}, device_id_type=MESH,
        )

    def rs_copy(u, s):
        return pltpu.make_async_remote_copy(
            src_ref=rss.at[u, s], dst_ref=rsr.at[u, s],
            send_sem=rs_s.at[u, s], recv_sem=rs_r.at[u, s],
            device_id={"tp": chip_at(s) * 2 + core}, device_id_type=MESH,
        )

    def ag_copy(c, s):
        return pltpu.make_async_remote_copy(
            src_ref=slopes[c].at[me], dst_ref=slopes[c].at[me],
            send_sem=ag_s.at[c, s], recv_sem=ag_r.at[c, s],
            device_id={"tp": chip_at(s) * 2 + core}, device_id_type=MESH,
        )

    def agd_copy(c, s):
        owner = chip_from(s) * 2 + core
        return pltpu.make_async_remote_copy(
            src_ref=slopes[c].at[owner], dst_ref=slopes[c].at[owner],
            send_sem=agd_s.at[c, s], recv_sem=agd_r.at[c, s],
            device_id={"tp": sibling}, device_id_type=MESH,
        )

    def ftoks(i):
        return pl.ds(pl.multiple_of(i * ftok, ftok), ftok)

    def f1_copy(i):
        to = lax.rem(me + i, NTP)
        return pltpu.make_async_remote_copy(
            src_ref=fpart.at[:, ftoks(to), :], dst_ref=frecv.at[i],
            send_sem=f1_s.at[i], recv_sem=f1_r.at[i],
            device_id={"tp": to}, device_id_type=MESH,
        )

    def f2_copy(i):
        to = lax.rem(me + i, NTP)
        return pltpu.make_async_remote_copy(
            src_ref=fslope.at[:, ftoks(me), :], dst_ref=fslope.at[:, ftoks(me), :],
            send_sem=f2_s.at[i], recv_sem=f2_r.at[i],
            device_id={"tp": to}, device_id_type=MESH,
        )

    def zpart(i):
        return pl.ds(pl.multiple_of(i * zrows, 16), zrows)

    def z1_copy(c, s):
        return pltpu.make_async_remote_copy(
            src_ref=drifts[c].at[zpart(lax.rem(rz + s, NZ)), :], dst_ref=zrecv.at[c, s],
            send_sem=z1_s.at[c, s], recv_sem=z1_r.at[c, s],
            device_id={"rep": rep_at(s)}, device_id_type=MESH,
        )

    def y_copy(c):
        return pltpu.make_async_remote_copy(
            src_ref=ysend.at[c], dst_ref=yrecv.at[c],
            send_sem=y_s.at[c], recv_sem=y_r.at[c],
            device_id={"rep": rz * 2 + 1 - ry}, device_id_type=MESH,
        )

    def z2_copy(c, s):
        return pltpu.make_async_remote_copy(
            src_ref=total.at[c, zpart(rz), :], dst_ref=total.at[c, zpart(rz), :],
            send_sem=z2_s.at[c, s], recv_sem=z2_r.at[c, s],
            device_id={"rep": rep_at(s)}, device_id_type=MESH,
        )

    def w_pair(c, s):
        q = chip_at(s)
        mine = w_v[(q * 2 + core) * 2 + c]
        other = w_v[(q * 2 + 1 - core) * 2 + c]
        return jnp.concatenate([mine, other], axis=1)

    def part_out(u, s, part):
        keep[u, s] = part[:, :LANES].astype(BF16)
        sibs[u, s] = part[:, LANES:].astype(BF16)
        sib_copy(u, s).start()

    def forward_one(c):
        def body(s):
            w_copy(c, s, 0).wait()
            w_copy(c, s, 1).wait()
            part_out(c, s, dot(h1[...], w_pair(c, s)))

        loop(0, NCHIP, body)

    def reduce_send(u):
        def body(s):
            sib_copy(u, s).wait_recv()
            rss[u, s] = (keep[u, s].astype(F32) + sibr[u, s].astype(F32)).astype(BF16)
            rs_copy(u, s).start()

        loop(1, NCHIP, body)

    def own_sum(u):
        sib_copy(u, 0).wait_recv()
        acc = keep[u, 0].astype(F32) + sibr[u, 0].astype(F32)
        for s in range(1, NCHIP):
            rs_copy(u, s).wait_recv()
            acc = acc + rsr[u, s].astype(F32)
        return acc

    def lanes(c):
        return pl.ds(c * LANES, LANES)

    def slope_send(c):
        diff = own_sum(c) - tgt[0, :, lanes(c)].astype(F32)
        slopes[c][me] = (diff * (1.0 / tokens)).astype(BF16)
        agd_copy(c, 0).start()
        loop(1, NCHIP, lambda s: ag_copy(c, s).start())

    def step_one_columns(c):
        slope = slopes[c]

        def body(s):
            q = chip_from(s)

            @pl.when(s > 0)
            def _():
                ag_copy(c, s).wait_recv()
                agd_copy(c, s).start()

            agd_copy(c, s).wait_recv()
            pair = jnp.concatenate([slope[q * 2 + core], slope[q * 2 + 1 - core]], axis=1)
            grad = dot(ht1[...], pair)
            mine = w_v[(q * 2 + core) * 2 + c]
            other = w_v[(q * 2 + 1 - core) * 2 + c]
            w = jnp.concatenate([mine, other], axis=1).astype(F32)
            ratio = grad * recip(jnp.abs(grad) + ADAM_EPS)
            cur = (w - INNER_RATE * (ratio + DECAY_RATE * w)).astype(BF16)
            t = lax.div(s, NX) * NX + lax.rem(NX - lax.rem(s, NX), NX)
            part_out(2 + c, t, dot(h2[...], cur))

        loop(0, NCHIP, body)

    def fragment_one(c):
        grad = dot(ht1[...], slopes[c][frag])
        anchor = w_v[frag * 2 + c].astype(F32)
        ratio = grad * recip(jnp.abs(grad) + ADAM_EPS)
        after = anchor - INNER_RATE * (ratio + DECAY_RATE * anchor)
        g1f[c] = grad
        synced[c] = after
        drifts[c][...] = (anchor - after).astype(BF16)
        loop(1, NZ, lambda s: z1_copy(c, s).start())
        part = dot(h2[...], after.astype(BF16))
        taken = jnp.where(frag == me, 1.0, 0.0) * tgt[1, :, lanes(c)].astype(F32)
        fpart[c] = (part - taken).astype(BF16)

    def z_sum(c):
        acc = drifts[c][zpart(rz), :].astype(F32)
        for s in range(1, NZ):
            z1_copy(c, s).wait_recv()
            acc = acc + zrecv[c, s].astype(F32)
        ysend[c] = acc.astype(BF16)
        y_copy(c).start()

    def y_sum(c):
        y_copy(c).wait_recv()
        total[c, zpart(rz), :] = (ysend[c].astype(F32) + yrecv[c].astype(F32)).astype(BF16)
        loop(1, NZ, lambda s: z2_copy(c, s).start())

    def fragment_slope():
        acc = fpart[:, ftoks(me), :].astype(F32)
        for i in range(1, NTP):
            f1_copy(i).wait_recv()
            acc = acc + frecv[i].astype(F32)
        fslope[:, ftoks(me), :] = (acc * (1.0 / tokens)).astype(BF16)
        loop(1, NTP, lambda i: f2_copy(i).start())

    def fragment_two():
        loop(1, NTP, lambda i: f2_copy(i).wait_recv())
        for c in range(2):
            grad = dot(ht2[...], fslope[c])
            one = g1f[c]
            first = BETA_ONE * (1.0 - BETA_ONE) * one + (1.0 - BETA_ONE) * grad
            second = BETA_TWO * (1.0 - BETA_TWO) * one * one + (1.0 - BETA_TWO) * grad * grad
            ratio = (first * (1.0 / (1.0 - BETA_ONE**2))) / (
                jnp.sqrt(second * (1.0 / (1.0 - BETA_TWO**2))) + ADAM_EPS
            )
            after = synced[c]
            final[c] = after - INNER_RATE * (ratio + DECAY_RATE * after)

    def residual_out(c):
        diff = own_sum(2 + c) - tgt[1, :, lanes(c)].astype(F32)
        res_ref[0, lanes(c), :] = diff.T

    def outer(c):
        loop(1, NZ, lambda s: z2_copy(c, s).wait_recv())
        anchor = w_v[frag * 2 + c].astype(F32)
        mean = total[c].astype(F32) * (1.0 / (2 * NZ))
        moved = OUTER_MOMENTUM * mom_v[:, lanes(c)] + mean
        new = anchor - OUTER_RATE * (mean + OUTER_MOMENTUM * moved)
        nm_ref[:, lanes(c)] = moved
        ng_ref[:, lanes(c)] = new
        lf_ref[0, :, lanes(c)] = (MIX_KEEP * final[c] + (1.0 - MIX_KEEP) * new).astype(BF16)

    forward_one(0)
    reduce_send(0)
    forward_one(1)
    reduce_send(1)
    ht1[...] = dot(pool_v[...], picks(0), 0, 0).astype(BF16)
    h2[...] = dot(picks(1), pool_v[...], 0, 0).astype(BF16)
    tpool_copy.wait()
    for k in range(2):
        tgt[k] = dot(picks(k), tpool_v[...], 0, 0).astype(BF16)
    slope_send(0)
    ht2[...] = dot(pool_v[...], picks(1), 0, 0).astype(BF16)
    slope_send(1)
    step_one_columns(0)
    reduce_send(2)
    fragment_one(0)
    step_one_columns(1)
    reduce_send(3)
    fragment_one(1)
    loop(1, NTP, lambda i: f1_copy(i).start())
    z_sum(0)
    fragment_slope()
    y_sum(0)
    residual_out(0)
    z_sum(1)
    fragment_two()
    y_sum(1)
    mom_copy.wait()
    outer(0)
    residual_out(1)
    outer(1)

    for u in range(4):
        loop(0, NCHIP, lambda s, u=u: sib_copy(u, s).wait_send())
        loop(1, NCHIP, lambda s, u=u: rs_copy(u, s).wait_send())
    for c in range(2):
        loop(1, NCHIP, lambda s, c=c: ag_copy(c, s).wait_send())
        loop(0, NCHIP, lambda s, c=c: agd_copy(c, s).wait_send())
        loop(1, NZ, lambda s, c=c: z1_copy(c, s).wait_send())
        y_copy(c).wait_send()
        loop(1, NZ, lambda s, c=c: z2_copy(c, s).wait_send())
    loop(1, NTP, lambda i: f1_copy(i).wait_send())
    loop(1, NTP, lambda i: f2_copy(i).wait_send())


def body(weights, hidden_pool, target_pool, token_rows, fragment, outer_momentum):
    depth, features = weights.shape
    pool = hidden_pool.shape[1]
    width = outer_momentum.shape[1]
    owned = target_pool.shape[2]
    tokens = token_rows.shape[2]
    zrows = depth // NZ
    blocks = features // LANES
    dma = pltpu.SemaphoreType.DMA
    scratch = [
        pltpu.VMEM((blocks, depth, LANES), BF16),
        pltpu.VMEM((pool, depth), BF16),
        pltpu.VMEM((pool, owned), BF16),
        pltpu.VMEM((depth, width), F32),
        pltpu.VMEM((tokens, depth), BF16),
        pltpu.VMEM((tokens, depth), BF16),
        pltpu.VMEM((depth, tokens), BF16),
        pltpu.VMEM((depth, tokens), BF16),
        pltpu.VMEM((2, tokens, owned), BF16),
        *[pltpu.VMEM((4, NCHIP, tokens, LANES), BF16)] * 5,
        *[pltpu.VMEM((NTP, tokens, LANES), BF16)] * 2,
        pltpu.VMEM((2, depth, LANES), F32),
        pltpu.VMEM((2, depth, LANES), F32),
        *[pltpu.VMEM((depth, LANES), BF16)] * 2,
        pltpu.VMEM((2, tokens, LANES), BF16),
        pltpu.VMEM((NTP, 2, tokens // NTP, LANES), BF16),
        pltpu.VMEM((2, tokens, LANES), BF16),
        pltpu.VMEM((2, depth, LANES), F32),
        pltpu.VMEM((2, NZ, zrows, LANES), BF16),
        pltpu.VMEM((2, zrows, LANES), BF16),
        pltpu.VMEM((2, zrows, LANES), BF16),
        pltpu.VMEM((2, depth, LANES), BF16),
        dma((2, NCHIP, 2)),
        dma((3,)),
        *[dma((4, NCHIP))] * 4,
        *[dma((2, NCHIP))] * 4,
        *[dma((NTP,))] * 4,
        dma((2, NZ)),
        dma((2, NZ)),
        dma((2,)),
        dma((2,)),
        dma((2, NZ)),
        dma((2, NZ)),
    ]
    hbm = pl.BlockSpec(memory_space=pl.ANY)
    vmem = pl.BlockSpec(memory_space=pltpu.VMEM)
    smem = pl.BlockSpec(memory_space=pltpu.SMEM)
    return pl.pallas_call(
        kernel,
        out_shape=(
            jax.ShapeDtypeStruct((depth, width), F32),
            jax.ShapeDtypeStruct((depth, width), F32),
            jax.ShapeDtypeStruct((1, depth, width), BF16),
            jax.ShapeDtypeStruct((1, owned, tokens), F32),
        ),
        in_specs=[hbm, hbm, hbm, vmem, smem, hbm],
        out_specs=(vmem, vmem, vmem, vmem),
        scratch_shapes=scratch,
        compiler_params=pltpu.CompilerParams(
            collective_id=0, has_side_effects=True, vmem_limit_bytes=56 * 1024 * 1024
        ),
    )(weights, hidden_pool, target_pool, token_rows[0], fragment, outer_momentum)


def solution(mesh):
    in_specs = (
        P("tp", None),
        P("rep", None, "tp"),
        P("rep", None, "tp"),
        P("rep", None, None),
        P(),
        P("tp", None),
    )
    out_specs = (P("tp", None), P("tp", None), P("rep", "tp", None), P("rep", "tp", None))
    return jax.shard_map(body, mesh=mesh, in_specs=in_specs, out_specs=out_specs, check_vma=False)
```

time: 430 us -> 97.2 us (0.23)
  the two profiles are of different devices: /device:TPU:2 before, /device:TPU:1 now
where the time goes in v1:
time: 97.2 us; the launch traced here: 97 us
  Pallas kernels  87.9 us (90%)
  local copies, waits for them, and re-layouts  7.8 us (8%)
  between operations  1.29 us (1%)
    pallas_call x1, Pallas kernels, body(): pl.pallas_call(kernel, out_shape=(jax.ShapeDtypeStruct((depth, width), F3...  87.9 us
    unnamed x4, local copies, waits for them, and re-layouts  7.8 us

profile of v1, /device:TPU:1, one launch (start us, length us, event | category | flops | bytes accessed | tf_op | source)
XLA Modules:
  0.0 97.0 jit_solution(7756411600934968762)
XLA Ops:
  1.3 87.9 %shard_map.93 = (f32[896,256]{1,0:T(8,128)}, f32[896,256]{1,0:T(8,128)}, bf16[1,896,256]{2,1,0:T(8,128)(2,1)}, f32[1,256,256]{2,1,0:T(8,128)}) custom-call(bf16[896,4096]{1,0:T(8,128)(2,1)} %w_hbm.1, bf16[1,512,896]{2,1,0:T(8,128)(2,1)} %pool_hbm.1, bf16[1,512,256]{2,1,0:T(8,128)(2,1)} %tpool_hbm.1, s32[2,256]{1,0:T(2,128)} %bitcast.1, s32[1]{0:T(128)S(6)} %copy.14.frag_ref, ...), custom_call_target="tpu_custom_call" | custom-call | tf_op jit(solution)/shard_map/pallas_call | solution.py:424
  89.1 2.2 %copy.15 = f32[896,256]{1,0:T(8,128)} copy(f32[896,256]{1,0:T(8,128)} %get-tuple-element.8) | data formatting | bytes 1835008
  91.3 2.2 %copy.16 = f32[896,256]{1,0:T(8,128)} copy(f32[896,256]{1,0:T(8,128)} %get-tuple-element.9) | data formatting | bytes 1835008
  93.5 1.8 %copy.17 = bf16[1,896,256]{2,1,0:T(8,128)(2,1)} copy(bf16[1,896,256]{2,1,0:T(8,128)(2,1)} %get-tuple-element.10) | data formatting | bytes 917504
  95.3 1.7 %copy.18 = f32[1,256,256]{2,1,0:T(8,128)} copy(f32[1,256,256]{2,1,0:T(8,128)} %get-tuple-element.11) | data formatting | bytes 524288

commit v2 on v1

--- a/solution.py
+++ b/solution.py
@@ -42,7 +42,7 @@
     w_v, pool_v, tpool_v, mom_v,
     h1, h2, ht1, ht2, tgt,
     keep, sibs, sibr, rss, rsr,
-    slope0, slope1,
+    slope0, slope1, grad0, grad1, cur0, cur1,
     g1f, synced, drift0, drift1, fpart, frecv, fslope, final,
     zrecv, ysend, yrecv, total,
     w_sem, in_sem,
@@ -67,12 +67,17 @@
     frag = frag_ref[0]
     slopes = (slope0, slope1)
     drifts = (drift0, drift1)
+    grads = (grad0, grad1)
+    currents = (cur0, cur1)
 
     def chip_at(s):
         return lax.rem(cy + lax.div(s, NX), 2) * NX + lax.rem(cx + lax.rem(s, NX), NX)
 
     def chip_from(s):
         return lax.rem(cy + lax.div(s, NX), 2) * NX + lax.rem(cx + NX - lax.rem(s, NX), NX)
+
+    def slot_of(s):
+        return s // NX * NX + (NX - s % NX) % NX
 
     def rep_at(s):
         return lax.rem(rz + s, NZ) * 2 + ry
@@ -207,18 +212,17 @@
         other = w_v[(q * 2 + 1 - core) * 2 + c]
         return jnp.concatenate([mine, other], axis=1)
 
-    def part_out(u, s, part):
-        keep[u, s] = part[:, :LANES].astype(BF16)
-        sibs[u, s] = part[:, LANES:].astype(BF16)
-        sib_copy(u, s).start()
-
     def forward_one(c):
-        def body(s):
-            w_copy(c, s, 0).wait()
-            w_copy(c, s, 1).wait()
-            part_out(c, s, dot(h1[...], w_pair(c, s)))
-
-        loop(0, NCHIP, body)
+        for s in range(0, NCHIP, 2):
+            for t in (s, s + 1):
+                w_copy(c, t, 0).wait()
+                w_copy(c, t, 1).wait()
+            for t in (s, s + 1):
+                part = dot(h1[...], w_pair(c, t))
+                keep[c, t] = part[:, :LANES].astype(BF16)
+                sibs[c, t] = part[:, LANES:].astype(BF16)
+            for t in (s, s + 1):
+                sib_copy(c, t).start()
 
     def reduce_send(u):
         def body(s):
@@ -248,26 +252,44 @@
     def step_one_columns(c):
         slope = slopes[c]
 
-        def body(s):
+        def gradient(s):
             q = chip_from(s)
-
-            @pl.when(s > 0)
-            def _():
-                ag_copy(c, s).wait_recv()
-                agd_copy(c, s).start()
-
-            agd_copy(c, s).wait_recv()
             pair = jnp.concatenate([slope[q * 2 + core], slope[q * 2 + 1 - core]], axis=1)
-            grad = dot(ht1[...], pair)
+            grads[s % 2][...] = dot(ht1[...], pair)
+
+        def adamw(s):
+            q = chip_from(s)
             mine = w_v[(q * 2 + core) * 2 + c]
             other = w_v[(q * 2 + 1 - core) * 2 + c]
             w = jnp.concatenate([mine, other], axis=1).astype(F32)
-            ratio = grad * recip(jnp.abs(grad) + ADAM_EPS)
-            cur = (w - INNER_RATE * (ratio + DECAY_RATE * w)).astype(BF16)
-            t = lax.div(s, NX) * NX + lax.rem(NX - lax.rem(s, NX), NX)
-            part_out(2 + c, t, dot(h2[...], cur))
-
-        loop(0, NCHIP, body)
+            grad = grads[s % 2][...]
+            scale = pl.reciprocal(jnp.abs(grad) * (1.0 / INNER_RATE) + ADAM_EPS / INNER_RATE, approx=True)
+            currents[s % 2][...] = (w * (1.0 - INNER_RATE * DECAY_RATE) - grad * scale).astype(BF16)
+
+        def forward_two(s):
+            t = slot_of(s)
+            part = dot(h2[...], currents[s % 2][...])
+            keep[2 + c, t] = part[:, :LANES].astype(BF16)
+            sibs[2 + c, t] = part[:, LANES:].astype(BF16)
+
+        for i in range(NCHIP + 2):
+            if i < NCHIP and c == 0:
+                agd_copy(c, i).wait_recv()
+            if i >= 2:
+                forward_two(i - 2)
+            if 1 <= i < NCHIP + 1:
+                adamw(i - 1)
+            if i < NCHIP:
+                gradient(i)
+            if i >= 2:
+                sib_copy(2 + c, slot_of(i - 2)).start()
+
+    def hand_over(c):
+        def body(s):
+            ag_copy(c, s).wait_recv()
+            agd_copy(c, s).start()
+
+        loop(1, NCHIP, body)
 
     def fragment_one(c):
         grad = dot(ht1[...], slopes[c][frag])
@@ -342,24 +364,27 @@
     slope_send(0)
     ht2[...] = dot(pool_v[...], picks(1), 0, 0).astype(BF16)
     slope_send(1)
+    hand_over(0)
     step_one_columns(0)
     reduce_send(2)
     fragment_one(0)
+    hand_over(1)
+    loop(0, NCHIP, lambda s: agd_copy(1, s).wait_recv())
+    fragment_one(1)
+    loop(1, NTP, lambda i: f1_copy(i).start())
     step_one_columns(1)
     reduce_send(3)
-    fragment_one(1)
-    loop(1, NTP, lambda i: f1_copy(i).start())
     z_sum(0)
     fragment_slope()
+    z_sum(1)
     y_sum(0)
+    y_sum(1)
+    fragment_two()
+    mom_copy.wait()
     residual_out(0)
-    z_sum(1)
-    fragment_two()
-    y_sum(1)
-    mom_copy.wait()
     outer(0)
+    outer(1)
     residual_out(1)
-    outer(1)
 
     for u in range(4):
         loop(0, NCHIP, lambda s, u=u: sib_copy(u, s).wait_send())
@@ -372,6 +397,15 @@
         loop(1, NZ, lambda s, c=c: z2_copy(c, s).wait_send())
     loop(1, NTP, lambda i: f1_copy(i).wait_send())
     loop(1, NTP, lambda i: f2_copy(i).wait_send())
+
+
+def copy_out(*refs):
+    sem = refs[-1]
+    copies = [pltpu.make_async_copy(refs[i], refs[4 + i], sem.at[i]) for i in range(4)]
+    for copy in copies:
+        copy.start()
+    for copy in copies:
+        copy.wait()
 
 
 def body(weights, hidden_pool, target_pool, token_rows, fragment, outer_momentum):
@@ -395,6 +429,8 @@
         pltpu.VMEM((2, tokens, owned), BF16),
         *[pltpu.VMEM((4, NCHIP, tokens, LANES), BF16)] * 5,
         *[pltpu.VMEM((NTP, tokens, LANES), BF16)] * 2,
+        *[pltpu.VMEM((depth, 2 * LANES), F32)] * 2,
+        *[pltpu.VMEM((depth, 2 * LANES), BF16)] * 2,
         pltpu.VMEM((2, depth, LANES), F32),
         pltpu.VMEM((2, depth, LANES), F32),
         *[pltpu.VMEM((depth, LANES), BF16)] * 2,
@@ -421,14 +457,15 @@
     hbm = pl.BlockSpec(memory_space=pl.ANY)
     vmem = pl.BlockSpec(memory_space=pltpu.VMEM)
     smem = pl.BlockSpec(memory_space=pltpu.SMEM)
-    return pl.pallas_call(
+    results = (
+        jax.ShapeDtypeStruct((depth, width), F32),
+        jax.ShapeDtypeStruct((depth, width), F32),
+        jax.ShapeDtypeStruct((1, depth, width), BF16),
+        jax.ShapeDtypeStruct((1, owned, tokens), F32),
+    )
+    held = pl.pallas_call(
         kernel,
-        out_shape=(
-            jax.ShapeDtypeStruct((depth, width), F32),
-            jax.ShapeDtypeStruct((depth, width), F32),
-            jax.ShapeDtypeStruct((1, depth, width), BF16),
-            jax.ShapeDtypeStruct((1, owned, tokens), F32),
-        ),
+        out_shape=tuple(pltpu.VMEM(r.shape, r.dtype) for r in results),
         in_specs=[hbm, hbm, hbm, vmem, smem, hbm],
         out_specs=(vmem, vmem, vmem, vmem),
         scratch_shapes=scratch,
@@ -436,6 +473,14 @@
             collective_id=0, has_side_effects=True, vmem_limit_bytes=56 * 1024 * 1024
         ),
     )(weights, hidden_pool, target_pool, token_rows[0], fragment, outer_momentum)
+    return pl.pallas_call(
+        copy_out,
+        out_shape=results,
+        in_specs=[hbm] * 4,
+        out_specs=(hbm,) * 4,
+        scratch_shapes=[dma((4,))],
+        compiler_params=pltpu.CompilerParams(vmem_limit_bytes=4 * 1024 * 1024),
+    )(*held)
 
 
 def solution(mesh):

time: 97.2 us -> 78.4 us (0.81)
  Pallas kernels: 87.9 us -> 75.8 us
  local copies, waits for them, and re-layouts: 7.8 us -> 0 us
    pallas_call x1 -> x2, Pallas kernels: 87.9 us -> 75.8 us  [the longest x1 74.3 us: body(): pl.pallas_call(kernel, out_shape=tuple((pltpu.VMEM(r.shape, r.dtype) for...]
    unnamed x4 -> x0, local copies, waits for them, and re-layouts: 7.8 us -> none
where the time goes in v2:
time: 78.4 us; the launch traced here: 77.3 us
  Pallas kernels  75.8 us (97%)
  between operations  1.45 us (2%)
    pallas_call x1, Pallas kernels, body(): pl.pallas_call(kernel, out_shape=tuple((pltpu.VMEM(r.shape, r.dtype) for...  74.3 us

profile of v2, /device:TPU:1, one launch (start us, length us, event | category | flops | bytes accessed | tf_op | source)
XLA Modules:
  0.0 77.3 jit_solution(11454166047748449318)
XLA Ops:
  1.3 74.3 %shard_map.93 = (f32[896,256]{1,0:T(8,128)S(1)}, f32[896,256]{1,0:T(8,128)S(1)}, bf16[1,896,256]{2,1,0:T(8,128)(2,1)S(1)}, f32[1,256,256]{2,1,0:T(8,128)S(1)}) custom-call(bf16[896,4096]{1,0:T(8,128)(2,1)} %w_hbm.1, bf16[1,512,896]{2,1,0:T(8,128)(2,1)} %pool_hbm.1, bf16[1,512,256]{2,1,0:T(8,128)(2,1)} %tpool_hbm.1, s32[2,256]{1,0:T(2,128)} %bitcast.1, ...), custom_call_target="tpu_custom_call" | custom-call | tf_op jit(solution)/shard_map/pallas_call | solution.py:466
  75.6 1.5 %shard_map.94 = (f32[896,256]{1,0:T(8,128)}, f32[896,256]{1,0:T(8,128)}, bf16[1,896,256]{2,1,0:T(8,128)(2,1)}, f32[1,256,256]{2,1,0:T(8,128)}) custom-call(f32[896,256]{1,0:T(8,128)S(1)} %get-tuple-element.8.refs_0_, f32[896,256]{1,0:T(8,128)S(1)} %get-tuple-element.9.refs_1_, bf16[1,896,256]{2,1,0:T(8,128)(2,1)S(1)} %get-tuple-element.10.refs_2_, ...), custom_call_target="tpu_custom_call" | custom-call | tf_op jit(solution)/shard_map/pallas_call | solution.py:476

commit v3 on v2

v3 whole, which is shorter than its diff:
```python
import functools

import jax
import jax.numpy as jnp
from jax import lax
from jax.experimental import pallas as pl
from jax.experimental.pallas import tpu as pltpu
from jax.sharding import PartitionSpec as P

BETA_ONE = 0.9
BETA_TWO = 0.95
INNER_RATE = 0.001
DECAY_RATE = 0.1
ADAM_EPS = 0.001
OUTER_RATE = 0.7
OUTER_MOMENTUM = 0.9
MIX_KEEP = 0.5

MESH = pl.DeviceIdType.MESH
F32 = jnp.float32
BF16 = jnp.bfloat16

NX = 4
NCHIP = 8
NTP = 16
NZ = 8
LANES = 128


def dot(a, b, ca=1, cb=0):
    return lax.dot_general(a, b, (((ca,), (cb,)), ((), ())), preferred_element_type=F32)


def recip(x):
    r = pl.reciprocal(x, approx=True)
    return r * (2.0 - x * r)


AHEAD, BEHIND, ACROSS = 1, NX - 1, NX
HOPS = (
    (6, None, AHEAD),
    (7, None, BEHIND),
    (2, None, BEHIND),
    (5, 0, ACROSS),
    (4, 1, ACROSS),
    (3, 2, BEHIND),
    (1, 3, AHEAD),
)
LAST_HOPS = (4, 5, 6)
SPREAD = (
    (0, AHEAD, 3),
    (0, BEHIND, 1),
    (0, ACROSS, 4),
    (1, ACROSS, 5),
    (4, AHEAD, 7),
    (3, AHEAD, 2),
    (5, BEHIND, 6),
)
OUTWARD = (6, 2, 7, 5, 4, 3, 1, 0)
GROUPS = (
    ((0, 0), (1, 0)),
    ((0, 1), (0, 3)),
    ((0, 4), (1, 1)),
    ((1, 3), (1, 4)),
    ((0, 5), (0, 7)),
    ((0, 2), (1, 5)),
    ((1, 7), (1, 2)),
    ((0, 6), (1, 6)),
)


def mirror(r):
    return r // NX * NX + (NX - r % NX) % NX


def kernel(
    w_hbm, pool_hbm, tpool_hbm, rows_ref, frag_ref, mom_hbm,
    nm_ref, ng_ref, lf_ref, res_ref,
    w_v, pool_v, tpool_v, mom_v,
    h1, h2, ht1, ht2, tgt,
    keep, sibs, sibr, rss, rsr,
    slope0, slope1, grad0, grad1, grad2, grad3, cur0, cur1, cur2, cur3,
    g1f, synced, drift0, drift1, fpart, frecv, fslope, final,
    zrecv, ysend, yrecv, total,
    w_sem, in_sem,
    sib_s, sib_r, rs_s, rs_r, ag_s, ag_r, agd_s, agd_r,
    f1_s, f1_r, f2_s, f2_r, z1_s, z1_r, y_s, y_r, z2_s, z2_r,
):
    tokens = rows_ref.shape[1]
    pool = pool_v.shape[0]
    depth = w_v.shape[1]
    zrows = depth // NZ
    ftok = tokens // NTP

    me = lax.axis_index("tp")
    core = lax.rem(me, 2)
    chip = lax.div(me, 2)
    cy = lax.div(chip, NX)
    cx = lax.rem(chip, NX)
    rep = lax.axis_index("rep")
    rz = lax.div(rep, 2)
    ry = lax.rem(rep, 2)
    sibling = chip * 2 + 1 - core
    frag = frag_ref[0]
    slopes = (slope0, slope1)
    drifts = (drift0, drift1)
    grads = (grad0, grad1, grad2, grad3)
    currents = (cur0, cur1, cur2, cur3)

    def chip_at(r):
        return lax.rem(cy + r // NX, 2) * NX + lax.rem(cx + r % NX * (1 + 2 * core), NX)

    def rep_at(s):
        return lax.rem(rz + s, NZ) * 2 + ry

    def loop(lo, hi, body):
        def step(i, carry):
            body(i)
            return carry

        lax.fori_loop(lo, hi, step, 0)

    def w_copy(c, r, j):
        slot = (chip_at(r) * 2 + j) * 2 + c
        return pltpu.make_async_copy(
            w_hbm.at[:, pl.ds(pl.multiple_of(slot * LANES, LANES), LANES)],
            w_v.at[slot],
            w_sem.at[c, r, j],
        )

    pool_copy = pltpu.make_async_copy(pool_hbm.at[0], pool_v, in_sem.at[0])
    tpool_copy = pltpu.make_async_copy(tpool_hbm.at[0], tpool_v, in_sem.at[1])
    mom_copy = pltpu.make_async_copy(mom_hbm, mom_v, in_sem.at[2])
    pool_copy.start()
    for c in range(2):
        for r in OUTWARD:
            w_copy(c, r, 0).start()
            w_copy(c, r, 1).start()
    tpool_copy.start()
    mom_copy.start()

    barrier = pltpu.get_barrier_semaphore()

    def greet_tp(i):
        pl.semaphore_signal(
            barrier, inc=1, device_id={"tp": lax.rem(me + i, NTP)}, device_id_type=MESH
        )

    def greet_z(i):
        pl.semaphore_signal(barrier, inc=1, device_id={"rep": rep_at(i)}, device_id_type=MESH)

    loop(1, NTP, greet_tp)
    loop(1, NZ, greet_z)
    pl.semaphore_signal(barrier, inc=1, device_id={"rep": rz * 2 + 1 - ry}, device_id_type=MESH)

    def picks(k):
        at = lax.broadcasted_iota(jnp.int32, (pool, tokens), 0)
        return jnp.where(at == rows_ref[pl.ds(k, 1), :], 1.0, 0.0).astype(BF16)

    pool_copy.wait()
    h1[...] = dot(picks(0), pool_v[...], 0, 0).astype(BF16)

    def sib_copy(u, r, to):
        return pltpu.make_async_remote_copy(
            src_ref=sibs.at[u, r], dst_ref=sibr.at[u, to],
            send_sem=sib_s.at[u, r], recv_sem=sib_r.at[u, to],
            device_id={"tp": sibling}, device_id_type=MESH,
        )

    def rs_copy(u, m):
        return pltpu.make_async_remote_copy(
            src_ref=rss.at[u, m], dst_ref=rsr.at[u, m],
            send_sem=rs_s.at[u, m], recv_sem=rs_r.at[u, m],
            device_id={"tp": chip_at(HOPS[m][2]) * 2 + core}, device_id_type=MESH,
        )

    def ag_copy(c, m):
        here, to, there = SPREAD[m]
        owner = chip_at(here) * 2 + core
        return pltpu.make_async_remote_copy(
            src_ref=slopes[c].at[owner], dst_ref=slopes[c].at[owner],
            send_sem=ag_s.at[c, m], recv_sem=ag_r.at[c, there],
            device_id={"tp": chip_at(to) * 2 + core}, device_id_type=MESH,
        )

    def ag_arrival(c, r):
        owner = chip_at(r) * 2 + core
        return pltpu.make_async_remote_copy(
            src_ref=slopes[c].at[owner], dst_ref=slopes[c].at[owner],
            send_sem=ag_s.at[c, 0], recv_sem=ag_r.at[c, r],
            device_id={"tp": sibling}, device_id_type=MESH,
        )

    def agd_copy(c, r):
        owner = chip_at(r) * 2 + core
        return pltpu.make_async_remote_copy(
            src_ref=slopes[c].at[owner], dst_ref=slopes[c].at[owner],
            send_sem=agd_s.at[c, r], recv_sem=agd_r.at[c, mirror(r)],
            device_id={"tp": sibling}, device_id_type=MESH,
        )

    def agd_arrival(c, r):
        owner = chip_at(r) * 2 + 1 - core
        return pltpu.make_async_remote_copy(
            src_ref=slopes[c].at[owner], dst_ref=slopes[c].at[owner],
            send_sem=agd_s.at[c, r], recv_sem=agd_r.at[c, r],
            device_id={"tp": sibling}, device_id_type=MESH,
        )

    def ftoks(i):
        return pl.ds(pl.multiple_of(i * ftok, ftok), ftok)

    def f1_copy(k, i):
        to = lax.rem(me + i, NTP)
        return pltpu.make_async_remote_copy(
            src_ref=fpart.at[k, :, ftoks(to), :], dst_ref=frecv.at[k, i],
            send_sem=f1_s.at[k, i], recv_sem=f1_r.at[k, i],
            device_id={"tp": to}, device_id_type=MESH,
        )

    def f2_copy(k, i):
        to = lax.rem(me + i, NTP)
        return pltpu.make_async_remote_copy(
            src_ref=fslope.at[k, :, ftoks(me), :], dst_ref=fslope.at[k, :, ftoks(me), :],
            send_sem=f2_s.at[k, i], recv_sem=f2_r.at[k, i],
            device_id={"tp": to}, device_id_type=MESH,
        )

    def zpart(i):
        return pl.ds(pl.multiple_of(i * zrows, 16), zrows)

    def z1_copy(c, s):
        return pltpu.make_async_remote_copy(
            src_ref=drifts[c].at[zpart(lax.rem(rz + s, NZ)), :], dst_ref=zrecv.at[c, s],
            send_sem=z1_s.at[c, s], recv_sem=z1_r.at[c, s],
            device_id={"rep": rep_at(s)}, device_id_type=MESH,
        )

    def y_copy(c):
        return pltpu.make_async_remote_copy(
            src_ref=ysend.at[c], dst_ref=yrecv.at[c],
            send_sem=y_s.at[c], recv_sem=y_r.at[c],
            device_id={"rep": rz * 2 + 1 - ry}, device_id_type=MESH,
        )

    def z2_copy(c, s):
        return pltpu.make_async_remote_copy(
            src_ref=total.at[c, zpart(rz), :], dst_ref=total.at[c, zpart(rz), :],
            send_sem=z2_s.at[c, s], recv_sem=z2_r.at[c, s],
            device_id={"rep": rep_at(s)}, device_id_type=MESH,
        )

    def lanes(c):
        return pl.ds(c * LANES, LANES)

    def w_pair(c, r):
        q = chip_at(r)
        mine = w_v[(q * 2 + core) * 2 + c]
        other = w_v[(q * 2 + 1 - core) * 2 + c]
        return jnp.concatenate([mine, other], axis=1)

    def hold(u, r, part):
        keep[u, r] = part[:, :LANES].astype(BF16)
        sibs[u, r] = part[:, LANES:].astype(BF16)

    def both(u, r):
        sib_copy(u, r, r).wait_recv()
        return keep[u, r].astype(F32) + sibr[u, r].astype(F32)

    def hop(u, m):
        r, added, _ = HOPS[m]
        acc = both(u, r)
        if added is not None:
            rs_copy(u, added).wait_recv()
            acc = acc + rsr[u, added].astype(F32)
        rss[u, m] = acc.astype(BF16)
        rs_copy(u, m).start()

    def hops(u, *messages):
        for m in messages:
            hop(u, m)

    def own_sum(u):
        acc = both(u, 0)
        for m in LAST_HOPS:
            rs_copy(u, m).wait_recv()
            acc = acc + rsr[u, m].astype(F32)
        return acc

    def forward_one(c, half):
        group = OUTWARD[half * 4 : half * 4 + 4]
        for r in group:
            w_copy(c, r, 0).wait()
            w_copy(c, r, 1).wait()
        for r in group:
            hold(c, r, dot(h1[...], w_pair(c, r)))
        if c == 0 and half == 0:
            pl.semaphore_wait(barrier, NTP - 1 + NZ)
        for r in group:
            sib_copy(c, r, mirror(r)).start()

    def slope_send(c):
        diff = own_sum(c) - tgt[0, :, lanes(c)].astype(F32)
        slopes[c][me] = (diff * (1.0 / tokens)).astype(BF16)
        for m in range(3):
            ag_copy(c, m).start()
        agd_copy(c, 0).start()

    def pass_on(c, *places):
        for r in places:
            ag_arrival(c, r).wait_recv()
            for m in range(3, len(SPREAD)):
                if SPREAD[m][0] == r:
                    ag_copy(c, m).start()
            agd_copy(c, r).start()

    def stage(i):
        if i < len(GROUPS):
            for c, r in GROUPS[i]:
                agd_arrival(c, r).wait_recv()
        if i >= 2:
            for j, (c, r) in enumerate(GROUPS[i - 2]):
                hold(2 + c, r, dot(h2[...], currents[i % 2 * 2 + j][...]))
        if 1 <= i <= len(GROUPS):
            for j, (c, r) in enumerate(GROUPS[i - 1]):
                at = (i - 1) % 2 * 2 + j
                w = w_pair(c, r).astype(F32)
                grad = grads[at][...]
                scale = pl.reciprocal(
                    jnp.abs(grad) * (1.0 / INNER_RATE) + ADAM_EPS / INNER_RATE, approx=True
                )
                now = w * (1.0 - INNER_RATE * DECAY_RATE) - grad * scale
                currents[at][...] = now.astype(BF16)
        if i < len(GROUPS):
            for j, (c, r) in enumerate(GROUPS[i]):
                q = chip_at(r)
                mine, other = slopes[c][q * 2 + core], slopes[c][q * 2 + 1 - core]
                grads[i % 2 * 2 + j][...] = dot(ht1[...], jnp.concatenate([mine, other], axis=1))
        if i >= 2:
            for c, r in GROUPS[i - 2]:
                sib_copy(2 + c, r, mirror(r)).start()

    def fragment_part(k, c, part):
        taken = jnp.where(frag == me, 1.0, 0.0) * tgt[k, :, lanes(c)].astype(F32)
        fpart[k, c] = (part - taken).astype(BF16)

    def fragment_forward():
        for c in range(2):
            fragment_part(0, c, dot(h1[...], w_v[frag * 2 + c]))
        loop(1, NTP, lambda i: f1_copy(0, i).start())

    def fragment_slope(k):
        acc = fpart[k, :, ftoks(me), :].astype(F32)
        for i in range(1, NTP):
            f1_copy(k, i).wait_recv()
            acc = acc + frecv[k, i].astype(F32)
        fslope[k, :, ftoks(me), :] = (acc * (1.0 / tokens)).astype(BF16)
        loop(1, NTP, lambda i: f2_copy(k, i).start())

    def fragment_one():
        loop(1, NTP, lambda i: f2_copy(0, i).wait_recv())
        for c in range(2):
            grad = dot(ht1[...], fslope[0, c])
            anchor = w_v[frag * 2 + c].astype(F32)
            ratio = grad * recip(jnp.abs(grad) + ADAM_EPS)
            after = anchor - INNER_RATE * (ratio + DECAY_RATE * anchor)
            g1f[c] = grad
            synced[c] = after
            drifts[c][...] = (anchor - after).astype(BF16)
            loop(1, NZ, lambda s, c=c: z1_copy(c, s).start())
        for c in range(2):
            fragment_part(1, c, dot(h2[...], synced[c].astype(BF16)))
        loop(1, NTP, lambda i: f1_copy(1, i).start())

    def fragment_two():
        loop(1, NTP, lambda i: f2_copy(1, i).wait_recv())
        for c in range(2):
            grad = dot(ht2[...], fslope[1, c])
            one = g1f[c]
            first = BETA_ONE * (1.0 - BETA_ONE) * one + (1.0 - BETA_ONE) * grad
            second = BETA_TWO * (1.0 - BETA_TWO) * one * one + (1.0 - BETA_TWO) * grad * grad
            ratio = (first * (1.0 / (1.0 - BETA_ONE**2))) / (
                jnp.sqrt(second * (1.0 / (1.0 - BETA_TWO**2))) + ADAM_EPS
            )
            after = synced[c]
            final[c] = after - INNER_RATE * (ratio + DECAY_RATE * after)

    def z_sum(c):
        acc = drifts[c][zpart(rz), :].astype(F32)
        for s in range(1, NZ):
            z1_copy(c, s).wait_recv()
            acc = acc + zrecv[c, s].astype(F32)
        ysend[c] = acc.astype(BF16)
        y_copy(c).start()

    def y_sum(c):
        y_copy(c).wait_recv()
        total[c, zpart(rz), :] = (ysend[c].astype(F32) + yrecv[c].astype(F32)).astype(BF16)
        loop(1, NZ, lambda s: z2_copy(c, s).start())

    def residual_out(c):
        diff = own_sum(2 + c) - tgt[1, :, lanes(c)].astype(F32)
        res_ref[0, lanes(c), :] = diff.T

    def outer(c):
        loop(1, NZ, lambda s: z2_copy(c, s).wait_recv())
        anchor = w_v[frag * 2 + c].astype(F32)
        mean = total[c].astype(F32) * (1.0 / (2 * NZ))
        moved = OUTER_MOMENTUM * mom_v[:, lanes(c)] + mean
        new = anchor - OUTER_RATE * (mean + OUTER_MOMENTUM * moved)
        nm_ref[:, lanes(c)] = moved
        ng_ref[:, lanes(c)] = new
        lf_ref[0, :, lanes(c)] = (MIX_KEEP * final[c] + (1.0 - MIX_KEEP) * new).astype(BF16)

    forward_one(0, 0)
    forward_one(0, 1)
    tpool_copy.wait()
    tgt[0] = dot(picks(0), tpool_v[...], 0, 0).astype(BF16)
    forward_one(1, 0)
    hops(0, 0, 2, 1)
    forward_one(1, 1)
    fragment_forward()
    hops(1, 0, 2, 1)
    ht1[...] = dot(pool_v[...], picks(0), 0, 0).astype(BF16)
    hops(0, 3, 4, 5)
    h2[...] = dot(picks(1), pool_v[...], 0, 0).astype(BF16)
    hops(1, 3, 4, 5)
    fragment_slope(0)
    tgt[1] = dot(picks(1), tpool_v[...], 0, 0).astype(BF16)
    hops(0, 6)
    hops(1, 6)
    ht2[...] = dot(pool_v[...], picks(1), 0, 0).astype(BF16)
    slope_send(0)
    slope_send(1)
    fragment_one()
    stage(0)
    pass_on(0, 1, 3, 4)
    pass_on(1, 1, 3, 4)
    stage(1)
    stage(2)
    pass_on(0, 5, 7, 2)
    pass_on(1, 5, 7, 2)
    stage(3)
    fragment_slope(1)
    stage(4)
    pass_on(0, 6)
    pass_on(1, 6)
    stage(5)
    stage(6)
    z_sum(0)
    stage(7)
    stage(8)
    stage(9)
    y_sum(0)
    hops(2, 2, 1)
    hops(3, 2, 1)
    z_sum(1)
    hops(2, 0)
    hops(3, 0)
    fragment_two()
    hops(2, 4, 5)
    hops(3, 4, 5)
    y_sum(1)
    hops(2, 3)
    hops(3, 3)
    mom_copy.wait()
    hops(2, 6)
    hops(3, 6)
    outer(0)
    residual_out(0)
    residual_out(1)
    outer(1)

    for u in range(4):
        for r in range(NCHIP):
            sib_copy(u, r, r).wait_send()
        for m in range(len(HOPS)):
            rs_copy(u, m).wait_send()
    for c in range(2):
        for m in range(len(SPREAD)):
            ag_copy(c, m).wait_send()
        for r in range(NCHIP):
            agd_copy(c, r).wait_send()
        loop(1, NZ, lambda s, c=c: z1_copy(c, s).wait_send())
        y_copy(c).wait_send()
        loop(1, NZ, lambda s, c=c: z2_copy(c, s).wait_send())
    for k in range(2):
        loop(1, NTP, lambda i, k=k: f1_copy(k, i).wait_send())
        loop(1, NTP, lambda i, k=k: f2_copy(k, i).wait_send())


def copy_out(*refs):
    sem = refs[-1]
    copies = [pltpu.make_async_copy(refs[i], refs[4 + i], sem.at[i]) for i in range(4)]
    for copy in copies:
        copy.start()
    for copy in copies:
        copy.wait()


def body(weights, hidden_pool, target_pool, token_rows, fragment, outer_momentum):
    depth, features = weights.shape
    pool = hidden_pool.shape[1]
    width = outer_momentum.shape[1]
    owned = target_pool.shape[2]
    tokens = token_rows.shape[2]
    zrows = depth // NZ
    blocks = features // LANES
    dma = pltpu.SemaphoreType.DMA
    scratch = [
        pltpu.VMEM((blocks, depth, LANES), BF16),
        pltpu.VMEM((pool, depth), BF16),
        pltpu.VMEM((pool, owned), BF16),
        pltpu.VMEM((depth, width), F32),
        pltpu.VMEM((tokens, depth), BF16),
        pltpu.VMEM((tokens, depth), BF16),
        pltpu.VMEM((depth, tokens), BF16),
        pltpu.VMEM((depth, tokens), BF16),
        pltpu.VMEM((2, tokens, owned), BF16),
        *[pltpu.VMEM((4, NCHIP, tokens, LANES), BF16)] * 5,
        *[pltpu.VMEM((NTP, tokens, LANES), BF16)] * 2,
        *[pltpu.VMEM((depth, 2 * LANES), F32)] * 4,
        *[pltpu.VMEM((depth, 2 * LANES), BF16)] * 4,
        pltpu.VMEM((2, depth, LANES), F32),
        pltpu.VMEM((2, depth, LANES), F32),
        *[pltpu.VMEM((depth, LANES), BF16)] * 2,
        pltpu.VMEM((2, 2, tokens, LANES), BF16),
        pltpu.VMEM((2, NTP, 2, tokens // NTP, LANES), BF16),
        pltpu.VMEM((2, 2, tokens, LANES), BF16),
        pltpu.VMEM((2, depth, LANES), F32),
        pltpu.VMEM((2, NZ, zrows, LANES), BF16),
        pltpu.VMEM((2, zrows, LANES), BF16),
        pltpu.VMEM((2, zrows, LANES), BF16),
        pltpu.VMEM((2, depth, LANES), BF16),
        dma((2, NCHIP, 2)),
        dma((3,)),
        *[dma((4, NCHIP))] * 4,
        *[dma((2, NCHIP))] * 4,
        *[dma((2, NTP))] * 4,
        dma((2, NZ)),
        dma((2, NZ)),
        dma((2,)),
        dma((2,)),
        dma((2, NZ)),
        dma((2, NZ)),
    ]
    hbm = pl.BlockSpec(memory_space=pl.ANY)
    vmem = pl.BlockSpec(memory_space=pltpu.VMEM)
    smem = pl.BlockSpec(memory_space=pltpu.SMEM)
    results = (
        jax.ShapeDtypeStruct((depth, width), F32),
        jax.ShapeDtypeStruct((depth, width), F32),
        jax.ShapeDtypeStruct((1, depth, width), BF16),
        jax.ShapeDtypeStruct((1, owned, tokens), F32),
    )
    held = pl.pallas_call(
        kernel,
        out_shape=tuple(pltpu.VMEM(r.shape, r.dtype) for r in results),
        in_specs=[hbm, hbm, hbm, vmem, smem, hbm],
        out_specs=(vmem, vmem, vmem, vmem),
        scratch_shapes=scratch,
        compiler_params=pltpu.CompilerParams(
            collective_id=0, has_side_effects=True, vmem_limit_bytes=56 * 1024 * 1024
        ),
    )(weights, hidden_pool, target_pool, token_rows[0], fragment, outer_momentum)
    return pl.pallas_call(
        copy_out,
        out_shape=results,
        in_specs=[hbm] * 4,
        out_specs=(hbm,) * 4,
        scratch_shapes=[dma((4,))],
        compiler_params=pltpu.CompilerParams(vmem_limit_bytes=4 * 1024 * 1024),
    )(*held)


def solution(mesh):
    in_specs = (
        P("tp", None),
        P("rep", None, "tp"),
        P("rep", None, "tp"),
        P("rep", None, None),
        P(),
        P("tp", None),
    )
    out_specs = (P("tp", None), P("tp", None), P("rep", "tp", None), P("rep", "tp", None))
    return jax.shard_map(body, mesh=mesh, in_specs=in_specs, out_specs=out_specs, check_vma=False)
```

time: 78.4 us -> 68.9 us (0.88)
  Pallas kernels: 75.8 us -> 66.3 us
    pallas_call x1, Pallas kernels: 74.3 us -> 64.8 us  [body(): pl.pallas_call(kernel, out_shape=tuple((pltpu.VMEM(r.shape, r.dtype) for...]
where the time goes in v3:
time: 68.9 us; the launch traced here: 67.7 us
  Pallas kernels  66.3 us (96%)
  between operations  1.45 us (2%)
    pallas_call x1, Pallas kernels, body(): pl.pallas_call(kernel, out_shape=tuple((pltpu.VMEM(r.shape, r.dtype) for...  64.8 us
    pallas_call x1, Pallas kernels, body(): pl.pallas_call(copy_out, out_shape=results, in_specs=[hbm] * 4, out_specs...  1.5 us

profile of v3, /device:TPU:1, one launch (start us, length us, event | category | flops | bytes accessed | tf_op | source)
XLA Modules:
  0.0 67.7 jit_solution(12687377101452591812)
XLA Ops:
  1.3 64.8 %shard_map.93 = (f32[896,256]{1,0:T(8,128)S(1)}, f32[896,256]{1,0:T(8,128)S(1)}, bf16[1,896,256]{2,1,0:T(8,128)(2,1)S(1)}, f32[1,256,256]{2,1,0:T(8,128)S(1)}) custom-call(bf16[896,4096]{1,0:T(8,128)(2,1)} %w_hbm.1, bf16[1,512,896]{2,1,0:T(8,128)(2,1)} %pool_hbm.1, bf16[1,512,256]{2,1,0:T(8,128)(2,1)} %tpool_hbm.1, s32[2,256]{1,0:T(2,128)} %bitcast.1, ...), custom_call_target="tpu_custom_call" | custom-call | tf_op jit(solution)/shard_map/pallas_call | solution.py:556
  66.0 1.5 %shard_map.94 = (f32[896,256]{1,0:T(8,128)}, f32[896,256]{1,0:T(8,128)}, bf16[1,896,256]{2,1,0:T(8,128)(2,1)}, f32[1,256,256]{2,1,0:T(8,128)}) custom-call(f32[896,256]{1,0:T(8,128)S(1)} %get-tuple-element.8.refs_0_, f32[896,256]{1,0:T(8,128)S(1)} %get-tuple-element.9.refs_1_, bf16[1,896,256]{2,1,0:T(8,128)(2,1)S(1)} %get-tuple-element.10.refs_2_, ...), custom_call_target="tpu_custom_call" | custom-call | tf_op jit(solution)/shard_map/pallas_call | solution.py:566

commit v4 on v3

--- a/solution.py
+++ b/solution.py
@@ -57,6 +57,7 @@
     (5, BEHIND, 6),
 )
 OUTWARD = (6, 2, 7, 5, 4, 3, 1, 0)
+FAR = 6
 GROUPS = (
     ((0, 0), (1, 0)),
     ((0, 1), (0, 3)),
@@ -167,9 +168,16 @@
             device_id={"tp": sibling}, device_id_type=MESH,
         )
 
+    def far_copy(u):
+        return pltpu.make_async_remote_copy(
+            src_ref=sibs.at[u, FAR], dst_ref=sibr.at[u, FAR],
+            send_sem=sib_s.at[u, FAR], recv_sem=sib_r.at[u, FAR],
+            device_id={"tp": chip_at(BEHIND) * 2 + 1 - core}, device_id_type=MESH,
+        )
+
     def rs_copy(u, m):
         return pltpu.make_async_remote_copy(
-            src_ref=rss.at[u, m], dst_ref=rsr.at[u, m],
+            src_ref=keep.at[u, FAR] if m == 0 else rss.at[u, m], dst_ref=rsr.at[u, m],
             send_sem=rs_s.at[u, m], recv_sem=rs_r.at[u, m],
             device_id={"tp": chip_at(HOPS[m][2]) * 2 + core}, device_id_type=MESH,
         )
@@ -197,6 +205,14 @@
             src_ref=slopes[c].at[owner], dst_ref=slopes[c].at[owner],
             send_sem=agd_s.at[c, r], recv_sem=agd_r.at[c, mirror(r)],
             device_id={"tp": sibling}, device_id_type=MESH,
+        )
+
+    def ag_far(c):
+        owner = chip_at(5) * 2 + core
+        return pltpu.make_async_remote_copy(
+            src_ref=slopes[c].at[owner], dst_ref=slopes[c].at[owner],
+            send_sem=agd_s.at[c, FAR], recv_sem=agd_r.at[c, FAR],
+            device_id={"tp": chip_at(BEHIND) * 2 + 1 - core}, device_id_type=MESH,
         )
 
     def agd_arrival(c, r):
@@ -267,9 +283,19 @@
         sib_copy(u, r, r).wait_recv()
         return keep[u, r].astype(F32) + sibr[u, r].astype(F32)
 
+    def send_partial(u, r):
+        if r == FAR:
+            rs_copy(u, 0).start()
+            far_copy(u).start()
+        else:
+            sib_copy(u, r, mirror(r)).start()
+
     def hop(u, m):
         r, added, _ = HOPS[m]
         acc = both(u, r)
+        if added == 0:
+            far_copy(u).wait_recv()
+            acc = acc + sibr[u, FAR].astype(F32)
         if added is not None:
             rs_copy(u, added).wait_recv()
             acc = acc + rsr[u, added].astype(F32)
@@ -297,7 +323,7 @@
         if c == 0 and half == 0:
             pl.semaphore_wait(barrier, NTP - 1 + NZ)
         for r in group:
-            sib_copy(c, r, mirror(r)).start()
+            send_partial(c, r)
 
     def slope_send(c):
         diff = own_sum(c) - tgt[0, :, lanes(c)].astype(F32)
@@ -312,7 +338,10 @@
             for m in range(3, len(SPREAD)):
                 if SPREAD[m][0] == r:
                     ag_copy(c, m).start()
-            agd_copy(c, r).start()
+            if r == 5:
+                ag_far(c).start()
+            if r != FAR:
+                agd_copy(c, r).start()
 
     def stage(i):
         if i < len(GROUPS):
@@ -338,7 +367,7 @@
                 grads[i % 2 * 2 + j][...] = dot(ht1[...], jnp.concatenate([mine, other], axis=1))
         if i >= 2:
             for c, r in GROUPS[i - 2]:
-                sib_copy(2 + c, r, mirror(r)).start()
+                send_partial(2 + c, r)
 
     def fragment_part(k, c, part):
         taken = jnp.where(frag == me, 1.0, 0.0) * tgt[k, :, lanes(c)].astype(F32)
@@ -417,37 +446,37 @@
     tpool_copy.wait()
     tgt[0] = dot(picks(0), tpool_v[...], 0, 0).astype(BF16)
     forward_one(1, 0)
-    hops(0, 0, 2, 1)
+    hops(0, 2, 1)
     forward_one(1, 1)
     fragment_forward()
-    hops(1, 0, 2, 1)
+    hops(1, 2, 1)
     ht1[...] = dot(pool_v[...], picks(0), 0, 0).astype(BF16)
     hops(0, 3, 4, 5)
+    fragment_slope(0)
+    hops(1, 3, 4, 5)
     h2[...] = dot(picks(1), pool_v[...], 0, 0).astype(BF16)
-    hops(1, 3, 4, 5)
-    fragment_slope(0)
     tgt[1] = dot(picks(1), tpool_v[...], 0, 0).astype(BF16)
     hops(0, 6)
     hops(1, 6)
-    ht2[...] = dot(pool_v[...], picks(1), 0, 0).astype(BF16)
+    fragment_one()
     slope_send(0)
     slope_send(1)
-    fragment_one()
+    ht2[...] = dot(pool_v[...], picks(1), 0, 0).astype(BF16)
     stage(0)
     pass_on(0, 1, 3, 4)
     pass_on(1, 1, 3, 4)
+    fragment_slope(1)
     stage(1)
     stage(2)
     pass_on(0, 5, 7, 2)
     pass_on(1, 5, 7, 2)
     stage(3)
-    fragment_slope(1)
+    z_sum(0)
     stage(4)
+    stage(5)
     pass_on(0, 6)
     pass_on(1, 6)
-    stage(5)
     stage(6)
-    z_sum(0)
     stage(7)
     stage(8)
     stage(9)
@@ -455,14 +484,10 @@
     hops(2, 2, 1)
     hops(3, 2, 1)
     z_sum(1)
-    hops(2, 0)
-    hops(3, 0)
     fragment_two()
-    hops(2, 4, 5)
-    hops(3, 4, 5)
+    hops(2, 3, 4, 5)
+    hops(3, 3, 4, 5)
     y_sum(1)
-    hops(2, 3)
-    hops(3, 3)
     mom_copy.wait()
     hops(2, 6)
     hops(3, 6)

time: 68.9 us -> 68.8 us (level); the launches traced: 67.7 us -> 68.4 us
  Pallas kernels: 66.3 us -> 67 us
    pallas_call x1, Pallas kernels: 64.8 us -> 65.5 us  [body(): pl.pallas_call(kernel, out_shape=tuple((pltpu.VMEM(r.shape, r.dtype) for...]
where the time goes in v4:
time: 68.8 us; the launch traced here: 68.4 us
  Pallas kernels  67 us (97%)
  between operations  1.45 us (2%)
    pallas_call x1, Pallas kernels, body(): pl.pallas_call(kernel, out_shape=tuple((pltpu.VMEM(r.shape, r.dtype) for...  65.5 us
    pallas_call x1, Pallas kernels, body(): pl.pallas_call(copy_out, out_shape=results, in_specs=[hbm] * 4, out_specs...  1.5 us

profile of v4, /device:TPU:1, one launch (start us, length us, event | category | flops | bytes accessed | tf_op | source)
XLA Modules:
  0.0 68.4 jit_solution(15587759533375198052)
XLA Ops:
  1.3 65.5 %shard_map.93 = (f32[896,256]{1,0:T(8,128)S(1)}, f32[896,256]{1,0:T(8,128)S(1)}, bf16[1,896,256]{2,1,0:T(8,128)(2,1)S(1)}, f32[1,256,256]{2,1,0:T(8,128)S(1)}) custom-call(bf16[896,4096]{1,0:T(8,128)(2,1)} %w_hbm.1, bf16[1,512,896]{2,1,0:T(8,128)(2,1)} %pool_hbm.1, bf16[1,512,256]{2,1,0:T(8,128)(2,1)} %tpool_hbm.1, s32[2,256]{1,0:T(2,128)} %bitcast.1, ...), custom_call_target="tpu_custom_call" | custom-call | tf_op jit(solution)/shard_map/pallas_call | solution.py:581
  66.8 1.5 %shard_map.94 = (f32[896,256]{1,0:T(8,128)}, f32[896,256]{1,0:T(8,128)}, bf16[1,896,256]{2,1,0:T(8,128)(2,1)}, f32[1,256,256]{2,1,0:T(8,128)}) custom-call(f32[896,256]{1,0:T(8,128)S(1)} %get-tuple-element.8.refs_0_, f32[896,256]{1,0:T(8,128)S(1)} %get-tuple-element.9.refs_1_, bf16[1,896,256]{2,1,0:T(8,128)(2,1)S(1)} %get-tuple-element.10.refs_2_, ...), custom_call_target="tpu_custom_call" | custom-call | tf_op jit(solution)/shard_map/pallas_call | solution.py:591

commit v5 on v4

--- a/solution.py
+++ b/solution.py
@@ -343,31 +343,59 @@
             if r != FAR:
                 agd_copy(c, r).start()
 
+    def columns_arrive(i):
+        for c, r in GROUPS[i]:
+            agd_arrival(c, r).wait_recv()
+
+    def columns_gradient(i):
+        for j, (c, r) in enumerate(GROUPS[i]):
+            q = chip_at(r)
+            mine, other = slopes[c][q * 2 + core], slopes[c][q * 2 + 1 - core]
+            grads[i % 2 * 2 + j][...] = dot(ht1[...], jnp.concatenate([mine, other], axis=1))
+
+    def columns_adamw(i):
+        for j, (c, r) in enumerate(GROUPS[i]):
+            at = i % 2 * 2 + j
+            w = w_pair(c, r).astype(F32)
+            grad = grads[at][...]
+            scale = pl.reciprocal(
+                jnp.abs(grad) * (1.0 / INNER_RATE) + ADAM_EPS / INNER_RATE, approx=True
+            )
+            now = w * (1.0 - INNER_RATE * DECAY_RATE) - grad * scale
+            currents[at][...] = now.astype(BF16)
+
+    def columns_forward(i):
+        for j, (c, r) in enumerate(GROUPS[i]):
+            hold(2 + c, r, dot(h2[...], currents[i % 2 * 2 + j][...]))
+
+    def columns_send(i):
+        for c, r in GROUPS[i]:
+            send_partial(2 + c, r)
+
     def stage(i):
-        if i < len(GROUPS):
-            for c, r in GROUPS[i]:
-                agd_arrival(c, r).wait_recv()
+        columns_arrive(i)
         if i >= 2:
-            for j, (c, r) in enumerate(GROUPS[i - 2]):
-                hold(2 + c, r, dot(h2[...], currents[i % 2 * 2 + j][...]))
-        if 1 <= i <= len(GROUPS):
-            for j, (c, r) in enumerate(GROUPS[i - 1]):
-                at = (i - 1) % 2 * 2 + j
-                w = w_pair(c, r).astype(F32)
-                grad = grads[at][...]
-                scale = pl.reciprocal(
-                    jnp.abs(grad) * (1.0 / INNER_RATE) + ADAM_EPS / INNER_RATE, approx=True
-                )
-                now = w * (1.0 - INNER_RATE * DECAY_RATE) - grad * scale
-                currents[at][...] = now.astype(BF16)
-        if i < len(GROUPS):
-            for j, (c, r) in enumerate(GROUPS[i]):
-                q = chip_at(r)
-                mine, other = slopes[c][q * 2 + core], slopes[c][q * 2 + 1 - core]
-                grads[i % 2 * 2 + j][...] = dot(ht1[...], jnp.concatenate([mine, other], axis=1))
+            columns_forward(i - 2)
+        if i >= 1:
+            columns_adamw(i - 1)
+        columns_gradient(i)
         if i >= 2:
-            for c, r in GROUPS[i - 2]:
-                send_partial(2 + c, r)
+            columns_send(i - 2)
+
+    def last_stages():
+        end = len(GROUPS) - 1
+        columns_forward(end - 2)
+        columns_adamw(end - 1)
+        columns_send(end - 2)
+        columns_forward(end - 1)
+        columns_send(end - 1)
+        pass_on(0, FAR)
+        pass_on(1, FAR)
+        columns_arrive(end)
+        columns_gradient(end)
+        columns_adamw(end)
+        columns_forward(end)
+        columns_send(end)
 
     def fragment_part(k, c, part):
         taken = jnp.where(frag == me, 1.0, 0.0) * tgt[k, :, lanes(c)].astype(F32)
@@ -440,6 +468,26 @@
         nm_ref[:, lanes(c)] = moved
         ng_ref[:, lanes(c)] = new
         lf_ref[0, :, lanes(c)] = (MIX_KEEP * final[c] + (1.0 - MIX_KEEP) * new).astype(BF16)
+
+    def sent(u):
+        for r in range(NCHIP):
+            sib_copy(u, r, r).wait_send()
+        for m in range(3):
+            rs_copy(u, m).wait_send()
+
+    def hops_sent(u):
+        for m in range(3, len(HOPS)):
+            rs_copy(u, m).wait_send()
+
+    def slopes_sent(c):
+        for m in range(len(SPREAD)):
+            ag_copy(c, m).wait_send()
+        for r in range(NCHIP):
+            agd_copy(c, r).wait_send()
+
+    def fragment_sent(k):
+        loop(1, NTP, lambda i: f1_copy(k, i).wait_send())
+        loop(1, NTP, lambda i: f2_copy(k, i).wait_send())
 
     forward_one(0, 0)
     forward_one(0, 1)
@@ -474,44 +522,40 @@
     z_sum(0)
     stage(4)
     stage(5)
-    pass_on(0, 6)
-    pass_on(1, 6)
     stage(6)
-    stage(7)
-    stage(8)
-    stage(9)
+    last_stages()
     y_sum(0)
     hops(2, 2, 1)
     hops(3, 2, 1)
     z_sum(1)
     fragment_two()
+    sent(0)
+    sent(1)
     hops(2, 3, 4, 5)
     hops(3, 3, 4, 5)
     y_sum(1)
     mom_copy.wait()
+    hops_sent(0)
+    hops_sent(1)
     hops(2, 6)
     hops(3, 6)
+    slopes_sent(0)
+    slopes_sent(1)
+    fragment_sent(0)
+    fragment_sent(1)
+    sent(2)
+    sent(3)
     outer(0)
     residual_out(0)
     residual_out(1)
     outer(1)
 
-    for u in range(4):
-        for r in range(NCHIP):
-            sib_copy(u, r, r).wait_send()
-        for m in range(len(HOPS)):
-            rs_copy(u, m).wait_send()
+    hops_sent(2)
+    hops_sent(3)
     for c in range(2):
-        for m in range(len(SPREAD)):
-            ag_copy(c, m).wait_send()
-        for r in range(NCHIP):
-            agd_copy(c, r).wait_send()
         loop(1, NZ, lambda s, c=c: z1_copy(c, s).wait_send())
         y_copy(c).wait_send()
         loop(1, NZ, lambda s, c=c: z2_copy(c, s).wait_send())
-    for k in range(2):
-        loop(1, NTP, lambda i, k=k: f1_copy(k, i).wait_send())
-        loop(1, NTP, lambda i, k=k: f2_copy(k, i).wait_send())
 
 
 def copy_out(*refs):

time: 68.8 us -> 67.6 us (0.983)
  Pallas kernels: 67 us -> 65.9 us
    pallas_call x1, Pallas kernels: 65.5 us -> 64.4 us  [body(): pl.pallas_call(kernel, out_shape=tuple((pltpu.VMEM(r.shape, r.dtype) for...]
where the time goes in v5:
time: 67.6 us; the launch traced here: 67.3 us
  Pallas kernels  65.9 us (97%)
  between operations  1.45 us (2%)
    pallas_call x1, Pallas kernels, body(): pl.pallas_call(kernel, out_shape=tuple((pltpu.VMEM(r.shape, r.dtype) for...  64.4 us
    pallas_call x1, Pallas kernels, body(): pl.pallas_call(copy_out, out_shape=results, in_specs=[hbm] * 4, out_specs...  1.5 us

profile of v5, /device:TPU:1, one launch (start us, length us, event | category | flops | bytes accessed | tf_op | source)
XLA Modules:
  0.0 67.3 jit_solution(12352222071770339422)
XLA Ops:
  1.3 64.4 %shard_map.93 = (f32[896,256]{1,0:T(8,128)S(1)}, f32[896,256]{1,0:T(8,128)S(1)}, bf16[1,896,256]{2,1,0:T(8,128)(2,1)S(1)}, f32[1,256,256]{2,1,0:T(8,128)S(1)}) custom-call(bf16[896,4096]{1,0:T(8,128)(2,1)} %w_hbm.1, bf16[1,512,896]{2,1,0:T(8,128)(2,1)} %pool_hbm.1, bf16[1,512,256]{2,1,0:T(8,128)(2,1)} %tpool_hbm.1, s32[2,256]{1,0:T(2,128)} %bitcast.1, ...), custom_call_target="tpu_custom_call" | custom-call | tf_op jit(solution)/shard_map/pallas_call | solution.py:625
  65.6 1.5 %shard_map.94 = (f32[896,256]{1,0:T(8,128)}, f32[896,256]{1,0:T(8,128)}, bf16[1,896,256]{2,1,0:T(8,128)(2,1)}, f32[1,256,256]{2,1,0:T(8,128)}) custom-call(f32[896,256]{1,0:T(8,128)S(1)} %get-tuple-element.8.refs_0_, f32[896,256]{1,0:T(8,128)S(1)} %get-tuple-element.9.refs_1_, bf16[1,896,256]{2,1,0:T(8,128)(2,1)S(1)} %get-tuple-element.10.refs_2_, ...), custom_call_target="tpu_custom_call" | custom-call | tf_op jit(solution)/shard_map/pallas_call | solution.py:635

commit v6 on v5

--- a/solution.py
+++ b/solution.py
@@ -313,11 +313,15 @@
             acc = acc + rsr[u, m].astype(F32)
         return acc
 
+    def w_arrive(c, half):
+        for r in OUTWARD[half * 4 : half * 4 + 4]:
+            w_copy(c, r, 0).wait()
+            w_copy(c, r, 1).wait()
+
     def forward_one(c, half):
         group = OUTWARD[half * 4 : half * 4 + 4]
-        for r in group:
-            w_copy(c, r, 0).wait()
-            w_copy(c, r, 1).wait()
+        if (c, half) != (1, 1):
+            w_arrive(c, half)
         for r in group:
             hold(c, r, dot(h1[...], w_pair(c, r)))
         if c == 0 and half == 0:
@@ -494,9 +498,10 @@
     tpool_copy.wait()
     tgt[0] = dot(picks(0), tpool_v[...], 0, 0).astype(BF16)
     forward_one(1, 0)
+    w_arrive(1, 1)
+    fragment_forward()
     hops(0, 2, 1)
     forward_one(1, 1)
-    fragment_forward()
     hops(1, 2, 1)
     ht1[...] = dot(pool_v[...], picks(0), 0, 0).astype(BF16)
     hops(0, 3, 4, 5)

time: 67.6 us -> 68.5 us (1.013)
  Pallas kernels: 65.9 us -> 67 us
    pallas_call x1, Pallas kernels: 64.4 us -> 65.5 us  [body(): pl.pallas_call(kernel, out_shape=tuple((pltpu.VMEM(r.shape, r.dtype) for...]
where the time goes in v6:
time: 68.5 us; the launch traced here: 68.4 us
  Pallas kernels  67 us (98%)
  between operations  1.45 us (2%)
    pallas_call x1, Pallas kernels, body(): pl.pallas_call(kernel, out_shape=tuple((pltpu.VMEM(r.shape, r.dtype) for...  65.5 us
    pallas_call x1, Pallas kernels, body(): pl.pallas_call(copy_out, out_shape=results, in_specs=[hbm] * 4, out_specs...  1.5 us

profile of v6, /device:TPU:1, one launch (start us, length us, event | category | flops | bytes accessed | tf_op | source)
XLA Modules:
  0.0 68.4 jit_solution(1911266175194567427)
XLA Ops:
  1.3 65.5 %shard_map.93 = (f32[896,256]{1,0:T(8,128)S(1)}, f32[896,256]{1,0:T(8,128)S(1)}, bf16[1,896,256]{2,1,0:T(8,128)(2,1)S(1)}, f32[1,256,256]{2,1,0:T(8,128)S(1)}) custom-call(bf16[896,4096]{1,0:T(8,128)(2,1)} %w_hbm.1, bf16[1,512,896]{2,1,0:T(8,128)(2,1)} %pool_hbm.1, bf16[1,512,256]{2,1,0:T(8,128)(2,1)} %tpool_hbm.1, s32[2,256]{1,0:T(2,128)} %bitcast.1, ...), custom_call_target="tpu_custom_call" | custom-call | tf_op jit(solution)/shard_map/pallas_call | solution.py:630
  66.8 1.5 %shard_map.94 = (f32[896,256]{1,0:T(8,128)}, f32[896,256]{1,0:T(8,128)}, bf16[1,896,256]{2,1,0:T(8,128)(2,1)}, f32[1,256,256]{2,1,0:T(8,128)}) custom-call(f32[896,256]{1,0:T(8,128)S(1)} %get-tuple-element.8.refs_0_, f32[896,256]{1,0:T(8,128)S(1)} %get-tuple-element.9.refs_1_, bf16[1,896,256]{2,1,0:T(8,128)(2,1)S(1)} %get-tuple-element.10.refs_2_, ...), custom_call_target="tpu_custom_call" | custom-call | tf_op jit(solution)/shard_map/pallas_call | solution.py:640
